TPU v7x, 128 devices: a whole 4x4x4 slice. The times are simulated.
128 devices in a mesh: tm: 16 (over z, x_lo, core), uly: 8 (over y, x_hi).
Axes of the slice: x: 4 (x_hi: 2, x_lo: 2; x = x_hi * 2 + x_lo), y: 4, z: 4, core: 2. Of those that a mesh axis runs over, the one named last changes fastest.
Arguments:
- queries: bfloat16 [12288, 5120], P(('tm', 'uly')), may hold values from -8 to 8
- keys: bfloat16 [12288, 5120], P(('tm', 'uly')), may hold values from -8 to 8
- values: bfloat16 [12288, 5120], P(('tm', 'uly')), may hold values from -6 to 6
- grad_out: bfloat16 [12288, 5120], P(('tm', 'uly')), may hold values from -6 to 6
Outputs:
- attended: bfloat16 [12288, 5120], P(('tm', 'uly'))
- grad_queries: bfloat16 [12288, 5120], P(('tm', 'uly'))
- grad_keys: bfloat16 [12288, 5120], P(('tm', 'uly'))
- grad_values: bfloat16 [12288, 5120], P(('tm', 'uly'))
All inputs are finite; a program needn't handle non-finite values.
Results may differ from a plain program's by a relative error of at most 0.0096.
Values may be sent and summed in bfloat16 or wider, within the bound.
No kernel may reach another device: no remote copies, remote signals or barrier semaphores. Data moves between devices by JAX's collectives and lax.ppermute only.
A program may use at most 192 MiB of HBM per device.

v0:
```python
import functools
import math

import jax
import jax.numpy as jnp
from jax import lax
from jax.experimental import pallas as pl
from jax.experimental.pallas import tpu as pltpu
from jax.sharding import Mesh
from jax.sharding import PartitionSpec as P

HEAD_DIM = 128
WINDOW = 5
ROWS = 96
ULY = 8
QUAD = 4
GROUP = ROWS * ULY
WIDE = HEAD_DIM + 16
FACTOR = HEAD_DIM ** -0.5
LOG2E = math.log2(math.e)
PLANE = ("xl", "co", "y", "xh")
COLUMN = ("y", "xh")
TIME = ("z", "xl", "co")
ALL = ("z", "xl", "co", "y", "xh")
BF = jnp.bfloat16
F32 = jnp.float32


def dot(a, b, ca=1, cb=0):
    return lax.dot_general(a, b, (((ca,), (cb,)), ((), ())), preferred_element_type=F32)


def attend(allowed, gi, q, g, od_ref, k_s, v_s, kt_s, vt_s, dk_s, dv_s, s_s, p_s):
    top = jnp.full((8, GROUP), -jnp.inf, F32)
    for c in range(WINDOW):
        s = dot(k_s[gi + c], q, 1, 1)
        s_s[c] = s
        best = jnp.max(s.reshape(GROUP // 8, 8, GROUP), axis=0)
        if c < WINDOW - 1:
            best = jnp.where(allowed(c), best, -jnp.inf)
        top = jnp.maximum(top, best)
    top = jnp.max(top, axis=0, keepdims=True)
    for c in range(WINDOW):
        base = top if c == WINDOW - 1 else jnp.where(allowed(c), top, 1e30)
        p_s[c] = jnp.exp2((s_s[c] - base) * (FACTOR * LOG2E)).astype(BF)
    out_t = dot(jnp.concatenate([vt_s[gi + c] for c in range(WINDOW)], axis=1), p_s[...].reshape(WINDOW * GROUP, GROUP))
    inv = 1.0 / out_t[HEAD_DIM:HEAD_DIM + 1]
    out_t = out_t[:HEAD_DIM] * inv
    g_t = g.astype(F32).T
    row_dot = jnp.sum(g_t * out_t, axis=0, keepdims=True) * inv
    g_tb = (g_t * inv).astype(BF)
    g_b = g_tb.T
    od_ref[:, 0] = blocks(out_t.T.astype(BF))
    dq_t = jnp.zeros((HEAD_DIM, GROUP), F32)
    dp = dot(v_s[gi], g_tb)
    for c in range(WINDOW):
        pb = p_s[c]
        ds = (pb.astype(F32) * (dp - row_dot)).astype(BF)
        if c < WINDOW - 1:
            dp = dot(v_s[gi + c + 1], g_tb)
            dv_s[gi + c] += dot(pb, g_b)
            dk_s[gi + c] += dot(ds, q)
        else:
            dv_s[gi + c] = dot(pb, g_b)
            dk_s[gi + c] = dot(ds, q)
        dq_t = dq_t + dot(kt_s[gi + c], ds)
    od_ref[:, 1] = blocks((dq_t * FACTOR).T.astype(BF))


def load_chunk(kv_ref, c, k_s, v_s, kt_s, vt_s):
    k, v = flat(kv_ref[:, 0]), flat(kv_ref[:, 1])
    k_s[c] = k
    v_s[c] = v
    kt_s[c] = k.T
    vt_s[c, :HEAD_DIM] = v.T
    vt_s[c, HEAD_DIM:] = jnp.ones((WIDE - HEAD_DIM, GROUP), BF)


def blocks(x):
    return x.reshape(ULY, ROWS, HEAD_DIM)


def flat(x):
    return x.reshape(GROUP, HEAD_DIM)


def main_kernel(pos_ref, qg_ref, prev_ref, own_ref, od_ref, back_k_ref, back_v_ref, mine_ref,
                k_s, v_s, kt_s, vt_s, dk_s, dv_s, s_s, p_s):
    gi = pl.program_id(0)
    z = pos_ref[0]

    @pl.when(gi == 0)
    def _():
        for c in range(QUAD):
            rows = slice(ULY * c, ULY * c + ULY)
            load_chunk(prev_ref.at[rows], c, k_s, v_s, kt_s, vt_s)
            load_chunk(own_ref.at[rows], QUAD + c, k_s, v_s, kt_s, vt_s)
        dk_s[:QUAD] = jnp.zeros((QUAD, GROUP, HEAD_DIM), F32)
        dv_s[:QUAD] = jnp.zeros((QUAD, GROUP, HEAD_DIM), F32)

    attend(lambda c: (z > 0) | (gi + c >= QUAD), gi, flat(qg_ref[:, 0]), flat(qg_ref[:, 1]), od_ref,
           k_s, v_s, kt_s, vt_s, dk_s, dv_s, s_s, p_s)
    back_k_ref[...] = blocks((dk_s[gi] * FACTOR).astype(BF))
    back_v_ref[...] = blocks(dv_s[gi].astype(BF))

    @pl.when(gi == QUAD - 1)
    def _():
        for c in range(QUAD):
            rows = slice(ULY * c, ULY * c + ULY)
            mine_ref[rows, 0] = blocks((dk_s[QUAD + c] * FACTOR).astype(BF))
            mine_ref[rows, 1] = blocks(dv_s[QUAD + c].astype(BF))


def fifth_kernel(flag_ref, all_ref, prev_ref, side_ref, core_ref, od_ref, mine_ref, b4_ref, b3_ref, b2_ref, b1_ref,
                 k_s, v_s, kt_s, vt_s, dk_s, dv_s, s_s, p_s):
    for c, ref in enumerate((prev_ref, side_ref, core_ref.at[0], core_ref.at[1], all_ref.at[:, 2:4])):
        load_chunk(ref, c, k_s, v_s, kt_s, vt_s)
    dk_s[:QUAD] = jnp.zeros((QUAD, GROUP, HEAD_DIM), F32)
    dv_s[:QUAD] = jnp.zeros((QUAD, GROUP, HEAD_DIM), F32)
    attend(lambda c: flag_ref[c] > 0, 0, flat(all_ref[:, 0]), flat(all_ref[:, 1]), od_ref,
           k_s, v_s, kt_s, vt_s, dk_s, dv_s, s_s, p_s)
    mine_ref[:, 0] = blocks(dk_s[WINDOW - 1] * FACTOR)
    mine_ref[:, 1] = blocks(dv_s[WINDOW - 1])
    far = jnp.where(flag_ref[4] == 0, 2, 3)
    for c, ref in ((0, b4_ref), (far, b3_ref), (1, b2_ref), (5 - far, b1_ref)):
        ref[:, 0] = blocks((dk_s[c] * FACTOR).astype(BF))
        ref[:, 1] = blocks(dv_s[c].astype(BF))


def scratch(chunks):
    return [
        pltpu.VMEM((chunks, GROUP, HEAD_DIM), BF),
        pltpu.VMEM((chunks, GROUP, HEAD_DIM), BF),
        pltpu.VMEM((chunks, HEAD_DIM, GROUP), BF),
        pltpu.VMEM((chunks, WIDE, GROUP), BF),
        pltpu.VMEM((chunks, GROUP, HEAD_DIM), F32),
        pltpu.VMEM((chunks, GROUP, HEAD_DIM), F32),
        pltpu.VMEM((WINDOW, GROUP, GROUP), F32),
        pltpu.VMEM((WINDOW, GROUP, GROUP), BF),
    ]


def cost(pairs):
    return pl.CostEstimate(flops=12 * pairs * GROUP * GROUP * HEAD_DIM,
                           bytes_accessed=pairs * 1000000, transcendentals=pairs * GROUP * GROUP)


def params(grid=False):
    return pltpu.CompilerParams(
        vmem_limit_bytes=56 * 2**20, dimension_semantics=("arbitrary",) if grid else None)


def bf(*dims):
    return jax.ShapeDtypeStruct((*dims, ROWS, HEAD_DIM), BF)


SMEM = pl.BlockSpec(memory_space=pltpu.SMEM)
VMEM = pl.BlockSpec(memory_space=pltpu.VMEM)
HBM = pl.BlockSpec(memory_space=pltpu.HBM)


def main_heads(pos, qg, prev, own):
    n = QUAD * ULY
    group = pl.BlockSpec((ULY, 2, ROWS, HEAD_DIM), lambda i: (i, 0, 0, 0))
    one = pl.BlockSpec((ULY, ROWS, HEAD_DIM), lambda i: (i, 0, 0))
    whole = pl.BlockSpec((n, 2, ROWS, HEAD_DIM), lambda i: (0, 0, 0, 0))
    return pl.pallas_call(
        main_kernel,
        out_shape=(bf(n, 2), bf(n), bf(n), bf(n, 2)),
        grid=(QUAD,),
        in_specs=[SMEM, group, whole, whole],
        out_specs=(group, one, one, whole),
        scratch_shapes=scratch(2 * QUAD),
        compiler_params=params(True),
        cost_estimate=cost(20),
        name="main_heads",
    )(pos, qg, prev, own)


def fifth_head(flags, mine, prev, side, core):
    return pl.pallas_call(
        fifth_kernel,
        out_shape=(bf(ULY, 2), jax.ShapeDtypeStruct((ULY, 2, ROWS, HEAD_DIM), F32)) + (bf(ULY, 2),) * 4,
        in_specs=[SMEM] + [VMEM] * 4,
        out_specs=(VMEM,) * 6,
        scratch_shapes=scratch(WINDOW),
        compiler_params=params(),
        cost_estimate=cost(5),
        name="fifth_head",
    )(flags, mine, prev, side, core)


def exchange(x, axes):
    return lax.all_to_all(x, axes, 0, 0, tiled=True)


def shifted(x, axes, size, distance):
    return lax.ppermute(x, axes, [(i - distance, i) for i in range(size) if 0 <= i - distance < size])


def pack_kernel(q_ref, g_ref, k_ref, v_ref, qg_ref, kv_ref):
    for i, ref in enumerate((q_ref, g_ref, k_ref, v_ref)):
        main_ref = qg_ref if i < 2 else kv_ref
        for u in range(ULY):
            for j in range(QUAD):
                col = (u * WINDOW + j) * HEAD_DIM
                main_ref[j * ULY + u, i % 2] = ref[:, col:col + HEAD_DIM]


def pack_fifth_kernel(q_ref, g_ref, k_ref, v_ref, fifth_ref, sem):
    copies = []
    for i, ref in enumerate((q_ref, g_ref, k_ref, v_ref)):
        for u in range(ULY):
            col = (u * WINDOW + QUAD) * HEAD_DIM
            copies.append(pltpu.make_async_copy(ref.at[:, pl.ds(col, HEAD_DIM)], fifth_ref.at[u, i], sem.at[i, u]))
    for copy in copies:
        copy.start()
    for copy in copies:
        copy.wait()


def unpack_kernel(first, main_ref, fifth_ref, *out_refs):
    for i, out_ref in enumerate(out_refs):
        for u in range(ULY):
            for j in range(WINDOW):
                col = (u * WINDOW + j) * HEAD_DIM
                out_ref[:, col:col + HEAD_DIM] = main_ref[j * ULY + u, i] if j < QUAD else fifth_ref[u, first + i]


def combine_kernel(mine_ref, k_ref, v_ref, out_ref):
    out_ref[:, 0] = (mine_ref[:, 0].astype(F32) + k_ref[...].astype(F32)).astype(BF)
    out_ref[:, 1] = (mine_ref[:, 1].astype(F32) + v_ref[...].astype(F32)).astype(BF)


def finish_kernel(od_ref, mine_ref, b4_ref, b3_ref, b2_ref, b1_ref, out_ref):
    out_ref[:, 0:2] = od_ref[...]
    total = mine_ref[...]
    for ref in (b4_ref, b3_ref, b2_ref, b1_ref):
        total = total + ref[...].astype(F32)
    out_ref[:, 2:4] = total.astype(BF)


def moved(kernel, name, out_shape, *arrays, limit=24):
    return pl.pallas_call(
        kernel,
        out_shape=tuple(out_shape),
        in_specs=[VMEM] * len(arrays),
        out_specs=(VMEM,) * len(out_shape),
        compiler_params=pltpu.CompilerParams(vmem_limit_bytes=limit * 2**20),
        cost_estimate=pl.CostEstimate(flops=0, bytes_accessed=2**22, transcendentals=0),
        name=name,
    )(*arrays)


def packed(*arrays):
    n = QUAD * ULY
    return moved(pack_kernel, "pack", [bf(n, 2)] * 2, *arrays, limit=56)


def packed_fifth(*arrays):
    return pl.pallas_call(
        pack_fifth_kernel,
        out_shape=bf(ULY, 4),
        in_specs=[HBM] * 4,
        out_specs=VMEM,
        scratch_shapes=[pltpu.SemaphoreType.DMA((4, ULY))],
        compiler_params=params(),
        cost_estimate=pl.CostEstimate(flops=0, bytes_accessed=2**21, transcendentals=0),
        name="pack_fifth",
    )(*arrays)


def unpacked(main, fifth, first):
    out = jax.ShapeDtypeStruct((ROWS, ULY * WINDOW * HEAD_DIM), BF)
    return moved(functools.partial(unpack_kernel, first), "unpack", [out] * 2, main, fifth)


def combined(*arrays):
    return moved(combine_kernel, "combine", [bf(QUAD * ULY, 2)], *arrays, limit=56)[0]


def swapped(x, axis):
    return lax.ppermute(x, axis, [(0, 1), (1, 0)])


def per_device(queries, keys, values, grad_out):
    z, xl, co = lax.axis_index("z"), lax.axis_index("xl"), lax.axis_index("co")
    fifth = exchange(packed_fifth(queries, grad_out, keys, values), COLUMN)
    qg, kv = packed(queries, grad_out, keys, values)
    fifth, kv = lax.optimization_barrier((fifth, kv))
    own = exchange(kv, PLANE)
    own5 = fifth[:, 2:4]
    prev5 = shifted(own5, "z", 4, 1)
    side5 = swapped(jnp.where(xl == 0, own5, prev5), "xl")
    core5 = swapped(jnp.stack([jnp.where(co == 0, own5, prev5), side5]), "co")
    later = (z > 0).astype(jnp.int32)
    side_ok, core_ok = jnp.maximum(later, xl), jnp.maximum(later, co)
    flags = jnp.stack([later, side_ok, core_ok, side_ok, co])
    own, qg = lax.optimization_barrier((own, qg))
    prev = shifted(own, "z", 4, 1)
    qg = exchange(qg, PLANE)

    od5, mine5, *back5 = fifth_head(flags, fifth, prev5, side5, core5)
    own, od5, mine5, *back5 = lax.optimization_barrier((own, od5, mine5, *back5))
    back5 = [shifted(part, TIME, 16, -d) for d, part in zip((4, 3, 2, 1), back5)]

    od, back_k, back_v, mine = main_heads(z.reshape(1), qg, prev, own)
    od, back_k, back_v, *back5 = lax.optimization_barrier((od, back_k, back_v, *back5))
    got_k = shifted(back_k, "z", 4, -1)
    got_v = shifted(back_v, "z", 4, -1)
    fifth = moved(finish_kernel, "finish", [bf(ULY, 4)], od5, mine5, *back5)[0]
    od, fifth = lax.optimization_barrier((od, fifth))
    od = exchange(od, PLANE)
    od, got_k, fifth, mine = lax.optimization_barrier((od, got_k, fifth, mine))
    fifth = exchange(fifth, COLUMN)
    fifth, dkv = lax.optimization_barrier((fifth, combined(mine, got_k, got_v)))
    dkv = exchange(dkv, PLANE)
    return (*unpacked(od, fifth, 0), *unpacked(dkv, fifth, 2))


def solution(mesh):
    fine = Mesh(mesh.devices.reshape(4, 2, 2, 4, 2), ALL)
    spec = P(ALL, None)
    return jax.shard_map(per_device, mesh=fine, in_specs=(spec,) * 4, out_specs=(spec,) * 4, check_vma=False)
```

profile of v0, /device:TPU:34, one launch (start us, length us, event | category | flops | bytes accessed | tf_op | source)
XLA Modules:
  0.0 212.1 jit_solution(12736303236624188879)
XLA Ops:
  0.6 2.3 %pack_fifth.1 = bf16[8,4,96,128]{3,2,1,0:T(8,128)(2,1)} custom-call(bf16[96,5120]{1,0:T(8,128)(2,1)} %q_ref.3, bf16[96,5120]{1,0:T(8,128)(2,1)} %g_ref.3, bf16[96,5120]{1,0:T(8,128)(2,1)} %k_ref.3, bf16[96,5120]{1,0:T(8,128)(2,1)} %v_ref.3), custom_call_target="tpu_custom_call" | custom-call | bytes 2097152 | tf_op jit(solution)/shard_map/pack_fifth/pallas_call | solution.py:261
  2.9 6.0 %all-to-all-start = ((bf16[8,4,96,128]{3,2,1,0:T(8,128)(2,1)}), bf16[8,4,96,128]{3,2,1,0:T(8,128)(2,1)S(1)}, u32[]{:S(2)}, u32[]{:S(2)}) async-start(bf16[8,4,96,128]{3,2,1,0:T(8,128)(2,1)} %pack_fifth.1), calls=%async_computation | async-start | bytes 1572864 | tf_op jit(solution)/shard_map/all_to_all | solution.py:194
  9.0 4.3 %pack.1 = (bf16[32,2,96,128]{3,2,1,0:T(8,128)(2,1)}, bf16[32,2,96,128]{3,2,1,0:T(8,128)(2,1)}) custom-call(bf16[96,5120]{1,0:T(8,128)(2,1)} %q_ref.3, bf16[96,5120]{1,0:T(8,128)(2,1)} %g_ref.3, bf16[96,5120]{1,0:T(8,128)(2,1)} %k_ref.3, bf16[96,5120]{1,0:T(8,128)(2,1)} %v_ref.3), custom_call_target="tpu_custom_call" | custom-call | bytes 4194304 | tf_op jit(solution)/shard_map/pack/pallas_call | solution.py:244
  13.2 10.1 %all-to-all-done.all_ref = bf16[8,4,96,128]{3,2,1,0:T(8,128)(2,1)S(1)} async-done(((bf16[8,4,96,128]{3,2,1,0:T(8,128)(2,1)}), bf16[8,4,96,128]{3,2,1,0:T(8,128)(2,1)S(1)}, u32[]{:S(2)}, u32[]{:S(2)}) %all-to-all-start) | async-done | bytes 786464 | tf_op jit(solution)/shard_map/all_to_all | solution.py:194
  23.4 5.2 %all-to-all-start.1 = ((bf16[32,2,96,128]{3,2,1,0:T(8,128)(2,1)}), bf16[32,2,96,128]{3,2,1,0:T(8,128)(2,1)S(1)}, u32[]{:S(2)}, u32[]{:S(2)}) async-start(bf16[32,2,96,128]{3,2,1,0:T(8,128)(2,1)} %get-tuple-element.47), calls=%async_computation.1 | async-start | bytes 3145728 | tf_op jit(solution)/shard_map/all_to_all | solution.py:194
  28.6 3.8 %collective-permute-start.1 = (bf16[8,2,96,128]{3,2,1,0:T(8,128)(2,1)S(1)}, bf16[8,2,96,128]{3,2,1,0:T(8,128)(2,1)S(1)}, u32[]{:S(2)}, u32[]{:S(2)}) collective-permute-start(bf16[8,2,96,128]{3,2,1,0:T(8,128)(2,1)S(1)} %slice.3), channel_id=1, source_target_pairs={{0,32},{32,64},{64,96},{1,33},{33,65},{65,97},{2,34},{34,66},{66,9... | collective-permute-start | bytes 1179656 | tf_op jit(solution)/shard_map/ppermute | solution.py:198
  32.4 9.2 %collective-permute-done.1.prev_ref = bf16[8,2,96,128]{3,2,1,0:T(8,128)(2,1)S(1)} collective-permute-done((bf16[8,2,96,128]{3,2,1,0:T(8,128)(2,1)S(1)}, bf16[8,2,96,128]{3,2,1,0:T(8,128)(2,1)S(1)}, u32[]{:S(2)}, u32[]{:S(2)}) %collective-permute-start.1) | collective-permute-done | bytes 393248 | tf_op jit(solution)/shard_map/ppermute | solution.py:198
  42.8 6.3 %all-to-all-done.1.own_ref = bf16[32,2,96,128]{3,2,1,0:T(8,128)(2,1)S(1)} async-done(((bf16[32,2,96,128]{3,2,1,0:T(8,128)(2,1)}), bf16[32,2,96,128]{3,2,1,0:T(8,128)(2,1)S(1)}, u32[]{:S(2)}, u32[]{:S(2)}) %all-to-all-start.1) | async-done | bytes 1572896 | tf_op jit(solution)/shard_map/all_to_all | solution.py:194
  49.1 3.8 %collective-permute-start = (bf16[32,2,96,128]{3,2,1,0:T(8,128)(2,1)S(1)}, bf16[32,2,96,128]{3,2,1,0:T(8,128)(2,1)}, u32[]{:S(2)}, u32[]{:S(2)}) collective-permute-start(bf16[32,2,96,128]{3,2,1,0:T(8,128)(2,1)S(1)} %all-to-all-done.1.own_ref), channel_id=1, source_target_pairs={{0,32},{32,64},{64,96},{1,33},{33,65},{65,97},{2,34},{34,66},{66,9... | collective-permute-start | bytes 4718600 | tf_op jit(solution)/shard_map/ppermute | solution.py:198
  52.9 7.9 %all-to-all-start.2 = ((bf16[32,2,96,128]{3,2,1,0:T(8,128)(2,1)}), bf16[32,2,96,128]{3,2,1,0:T(8,128)(2,1)}, u32[]{:S(2)}, u32[]{:S(2)}) async-start(bf16[32,2,96,128]{3,2,1,0:T(8,128)(2,1)} %get-tuple-element.49), calls=%async_computation.2 | async-start | bytes 3145728 | tf_op jit(solution)/shard_map/all_to_all | solution.py:194
  64.4 12.5 %fifth_head.1 = (bf16[8,2,96,128]{3,2,1,0:T(8,128)(2,1)}, f32[8,2,96,128]{3,2,1,0:T(8,128)}, bf16[8,2,96,128]{3,2,1,0:T(8,128)(2,1)}, bf16[8,2,96,128]{3,2,1,0:T...) custom-call(s32[5]{0:T(128)} %stack.29.flag_ref, bf16[8,4,96,128]{3,2,1,0:T(8,128)(2,1)} %copy-done.2, ...), custom_call_target="tpu_custom_call" | custom-call | flops 4529848320 | bytes 5000000 | tf_op jit(solution)/shard_map/fifth_head/pallas_call | solution.py:181
  76.9 3.1 %collective-permute-start.4 = (bf16[8,2,96,128]{3,2,1,0:T(8,128)(2,1)}, bf16[8,2,96,128]{3,2,1,0:T(8,128)(2,1)S(1)}, u32[]{:S(2)}, u32[]{:S(2)}) collective-permute-start(bf16[8,2,96,128]{3,2,1,0:T(8,128)(2,1)} %get-tuple-element.62), channel_id=1, source_target_pairs={{32,0},{40,8},{48,16},{56,24},{64,32},{72,40},{80,48},{88,56},{96,... | collective-permute-start | bytes 1179656 | tf_op jit(solution)/shard_map/ppermute | solution.py:198
  82.0 2.2 %collective-permute-start.6 = (bf16[8,2,96,128]{3,2,1,0:T(8,128)(2,1)}, bf16[8,2,96,128]{3,2,1,0:T(8,128)(2,1)S(1)}, u32[]{:S(2)}, u32[]{:S(2)}) collective-permute-start(bf16[8,2,96,128]{3,2,1,0:T(8,128)(2,1)} %get-tuple-element.64), channel_id=1, source_target_pairs={{16,0},{24,8},{32,16},{40,24},{48,32},{56,40},{64,48},{72,56},{80,... | collective-permute-start | bytes 1179656 | tf_op jit(solution)/shard_map/ppermute | solution.py:198
  84.2 2.4 %collective-permute-start.7 = (bf16[8,2,96,128]{3,2,1,0:T(8,128)(2,1)}, bf16[8,2,96,128]{3,2,1,0:T(8,128)(2,1)S(1)}, u32[]{:S(2)}, u32[]{:S(2)}) collective-permute-start(bf16[8,2,96,128]{3,2,1,0:T(8,128)(2,1)} %get-tuple-element.65), channel_id=1, source_target_pairs={{8,0},{16,8},{24,16},{32,24},{40,32},{48,40},{56,48},{64,56},{72,6... | collective-permute-start | bytes 1179656 | tf_op jit(solution)/shard_map/ppermute | solution.py:198
  88.2 42.4 %main_heads.1 = (bf16[32,2,96,128]{3,2,1,0:T(8,128)(2,1)}, bf16[32,96,128]{2,1,0:T(8,128)(2,1)}, bf16[32,96,128]{2,1,0:T(8,128)(2,1)}, bf16[32,2,96,128]{3,2,1,0:T(8,128)(2,1)}) custom-call(s32[1]{0:T(128)} %bitcast.pos_ref, bf16[32,2,96,128]{3,2,1,0:T(8,128)(2,1)} %all-to-all-done.2.qg_ref, bf16[32,2,96,128]{3,2,1,0:T(8,128)(2,1)} %collective-permute-done.prev_ref, ...), custom_call_target="tpu_custom_call" | custom-call | flops 18119393280 | bytes 20000000 | tf_op jit(solution)/shard_map/main_heads/pallas_call | solution.py:167
  131.9 6.1 %all-to-all-start.3 = ((bf16[32,2,96,128]{3,2,1,0:T(8,128)(2,1)}), bf16[32,2,96,128]{3,2,1,0:T(8,128)(2,1)S(1)}, u32[]{:S(2)}, u32[]{:S(2)}) async-start(bf16[32,2,96,128]{3,2,1,0:T(8,128)(2,1)} %get-tuple-element.73), calls=%async_computation.3 | async-start | bytes 3145728 | tf_op jit(solution)/shard_map/all_to_all | solution.py:194
  139.9 1.9 collective-permute-start.9
  141.9 19.0 %collective-permute-done.8.k_ref = bf16[32,96,128]{2,1,0:T(8,128)(2,1)S(1)} collective-permute-done((bf16[32,96,128]{2,1,0:T(8,128)(2,1)S(1)}, bf16[32,96,128]{2,1,0:T(8,128)(2,1)S(1)}, u32[]{:S(2)}, u32[]{:S(2)}) %collective-permute-start.8) | collective-permute-done | bytes 786464 | tf_op jit(solution)/shard_map/ppermute | solution.py:198
  160.9 5.8 %all-to-all-start.4 = ((bf16[8,4,96,128]{3,2,1,0:T(8,128)(2,1)}), bf16[8,4,96,128]{3,2,1,0:T(8,128)(2,1)S(1)}, u32[]{:S(2)}, u32[]{:S(2)}) async-start(bf16[8,4,96,128]{3,2,1,0:T(8,128)(2,1)} %finish.1), calls=%async_computation.4 | async-start | bytes 1572864 | tf_op jit(solution)/shard_map/all_to_all | solution.py:194
  166.7 10.7 %collective-permute-done.9.v_ref = bf16[32,96,128]{2,1,0:T(8,128)(2,1)} collective-permute-done((bf16[32,96,128]{2,1,0:T(8,128)(2,1)}, bf16[32,96,128]{2,1,0:T(8,128)(2,1)}, u32[]{:S(2)}, u32[]{:S(2)}) %collective-permute-start.9) | collective-permute-done | bytes 786464 | tf_op jit(solution)/shard_map/ppermute | solution.py:198
  177.4 3.4 %combine.1 = bf16[32,2,96,128]{3,2,1,0:T(8,128)(2,1)} custom-call(bf16[32,2,96,128]{3,2,1,0:T(8,128)(2,1)} %get-tuple-element.79.mine_ref, bf16[32,96,128]{2,1,0:T(8,128)(2,1)} %copy-done.4, bf16[32,96,128]{2,1,0:T(8,128)(2,1)} %collective-permute-done.9.v_ref), custom_call_target="tpu_custom_call" | custom-call | bytes 4194304 | tf_op jit(solution)/shard_map/combine/pallas_call | solution.py:244
  180.8 7.4 %all-to-all-start.5 = ((bf16[32,2,96,128]{3,2,1,0:T(8,128)(2,1)}), bf16[32,2,96,128]{3,2,1,0:T(8,128)(2,1)}, u32[]{:S(2)}, u32[]{:S(2)}) async-start(bf16[32,2,96,128]{3,2,1,0:T(8,128)(2,1)} %combine.1), calls=%async_computation.5 | async-start | bytes 3145728 | tf_op jit(solution)/shard_map/all_to_all | solution.py:194
  189.9 19.0 %all-to-all-done.5.main_ref = bf16[32,2,96,128]{3,2,1,0:T(8,128)(2,1)} async-done(((bf16[32,2,96,128]{3,2,1,0:T(8,128)(2,1)}), bf16[32,2,96,128]{3,2,1,0:T(8,128)(2,1)}, u32[]{:S(2)}, u32[]{:S(2)}) %all-to-all-start.5) | async-done | bytes 1572896 | tf_op jit(solution)/shard_map/all_to_all | solution.py:194
  208.9 3.1 %unpack.3 = (bf16[96,5120]{1,0:T(8,128)(2,1)}, bf16[96,5120]{1,0:T(8,128)(2,1)}) custom-call(bf16[32,2,96,128]{3,2,1,0:T(8,128)(2,1)} %all-to-all-done.5.main_ref, bf16[8,4,96,128]{3,2,1,0:T(8,128)(2,1)S(1)} %all-to-all-done.4.fifth_ref), custom_call_target="tpu_custom_call" | custom-call | bytes 4194304 | tf_op jit(solution)/shard_map/unpack/pallas_call | solution.py:244
  (38 shorter events, 13.1 us)
Async XLA Ops:
  2.9 20.4 %all-to-all-start = ((bf16[8,4,96,128]{3,2,1,0:T(8,128)(2,1)}), bf16[8,4,96,128]{3,2,1,0:T(8,128)(2,1)S(1)}, u32[]{:S(2)}, u32[]{:S(2)}) async-start(bf16[8,4,96,128]{3,2,1,0:T(8,128)(2,1)} %pack_fifth.1), calls=%async_computation | async-start | bytes 1572864 | tf_op jit(solution)/shard_map/all_to_all | solution.py:194
  23.4 18.3 %copy-start.2 = (bf16[8,4,96,128]{3,2,1,0:T(8,128)(2,1)}, bf16[8,4,96,128]{3,2,1,0:T(8,128)(2,1)S(1)}, u32[]{:S(2)}) copy-start(bf16[8,4,96,128]{3,2,1,0:T(8,128)(2,1)S(1)} %all-to-all-done.all_ref) | copy-start | bytes 2359300
  23.4 25.8 %all-to-all-start.1 = ((bf16[32,2,96,128]{3,2,1,0:T(8,128)(2,1)}), bf16[32,2,96,128]{3,2,1,0:T(8,128)(2,1)S(1)}, u32[]{:S(2)}, u32[]{:S(2)}) async-start(bf16[32,2,96,128]{3,2,1,0:T(8,128)(2,1)} %get-tuple-element.47), calls=%async_computation.1 | async-start | bytes 3145728 | tf_op jit(solution)/shard_map/all_to_all | solution.py:194
  28.6 13.1 %collective-permute-start.1 = (bf16[8,2,96,128]{3,2,1,0:T(8,128)(2,1)S(1)}, bf16[8,2,96,128]{3,2,1,0:T(8,128)(2,1)S(1)}, u32[]{:S(2)}, u32[]{:S(2)}) collective-permute-start(bf16[8,2,96,128]{3,2,1,0:T(8,128)(2,1)S(1)} %slice.3), channel_id=1, source_target_pairs={{0,32},{32,64},{64,96},{1,33},{33,65},{65,97},{2,34},{34,66},{66,9... | collective-permute-start | bytes 1179656 | tf_op jit(solution)/shard_map/ppermute | solution.py:198
  41.6 11.3 %copy-start.5 = (bf16[8,2,96,128]{3,2,1,0:T(8,128)(2,1)}, bf16[8,2,96,128]{3,2,1,0:T(8,128)(2,1)S(1)}, u32[]{:S(2)}) copy-start(bf16[8,2,96,128]{3,2,1,0:T(8,128)(2,1)S(1)} %collective-permute-done.1.prev_ref) | copy-start | bytes 1179652
  42.5 18.3 %collective-permute-start.2 = (bf16[8,2,96,128]{3,2,1,0:T(8,128)(2,1)}, bf16[8,2,96,128]{3,2,1,0:T(8,128)(2,1)S(1)}, u32[]{:S(2)}, u32[]{:S(2)}) collective-permute-start(bf16[8,2,96,128]{3,2,1,0:T(8,128)(2,1)} %get-tuple-element.89), channel_id=1, source_target_pairs={{0,16},{16,0},{1,17},{17,1},{2,18},{18,2},{3,19},{19,3},{4,20},{20... | collective-permute-start | bytes 1179656 | tf_op jit(solution)/shard_map/ppermute | solution.py:283
  49.1 3.8 %copy-start.3 = (bf16[32,2,96,128]{3,2,1,0:T(8,128)(2,1)}, bf16[32,2,96,128]{3,2,1,0:T(8,128)(2,1)S(1)}, u32[]{:S(2)}) copy-start(bf16[32,2,96,128]{3,2,1,0:T(8,128)(2,1)S(1)} %all-to-all-done.1.own_ref) | copy-start | bytes 4718596
  49.1 39.1 %collective-permute-start = (bf16[32,2,96,128]{3,2,1,0:T(8,128)(2,1)S(1)}, bf16[32,2,96,128]{3,2,1,0:T(8,128)(2,1)}, u32[]{:S(2)}, u32[]{:S(2)}) collective-permute-start(bf16[32,2,96,128]{3,2,1,0:T(8,128)(2,1)S(1)} %all-to-all-done.1.own_ref), channel_id=1, source_target_pairs={{0,32},{32,64},{64,96},{1,33},{33,65},{65,97},{2,34},{34,66},{66,9... | collective-permute-start | bytes 4718600 | tf_op jit(solution)/shard_map/ppermute | solution.py:198
  52.9 33.7 %all-to-all-start.2 = ((bf16[32,2,96,128]{3,2,1,0:T(8,128)(2,1)}), bf16[32,2,96,128]{3,2,1,0:T(8,128)(2,1)}, u32[]{:S(2)}, u32[]{:S(2)}) async-start(bf16[32,2,96,128]{3,2,1,0:T(8,128)(2,1)} %get-tuple-element.49), calls=%async_computation.2 | async-start | bytes 3145728 | tf_op jit(solution)/shard_map/all_to_all | solution.py:194
  60.9 2.6 %copy-start.6 = (bf16[8,2,96,128]{3,2,1,0:T(8,128)(2,1)}, bf16[8,2,96,128]{3,2,1,0:T(8,128)(2,1)S(1)}, u32[]{:S(2)}) copy-start(bf16[8,2,96,128]{3,2,1,0:T(8,128)(2,1)S(1)} %collective-permute-done.2.side_ref) | copy-start | bytes 1179652
  61.0 2.5 %collective-permute-start.3 = (bf16[2,8,2,96,128]{4,3,2,1,0:T(8,128)(2,1)S(1)}, bf16[2,8,2,96,128]{4,3,2,1,0:T(8,128)(2,1)S(1)}, u32[]{:S(2)}, u32[]{:S(2)}) collective-permute-start(bf16[2,8,2,96,128]{4,3,2,1,0:T(8,128)(2,1)S(1)} %pad_maximum_fusion), channel_id=1, source_target_pairs={{0,8},{8,0},{1,9},{9,1},{2,10},{10,2},{3,11},{11,3},{4,12},{12,4},... | collective-permute-start | bytes 2359304 | tf_op jit(solution)/shard_map/ppermute | solution.py:283
  76.9 53.8 %collective-permute-start.4 = (bf16[8,2,96,128]{3,2,1,0:T(8,128)(2,1)}, bf16[8,2,96,128]{3,2,1,0:T(8,128)(2,1)S(1)}, u32[]{:S(2)}, u32[]{:S(2)}) collective-permute-start(bf16[8,2,96,128]{3,2,1,0:T(8,128)(2,1)} %get-tuple-element.62), channel_id=1, source_target_pairs={{32,0},{40,8},{48,16},{56,24},{64,32},{72,40},{80,48},{88,56},{96,... | collective-permute-start | bytes 1179656 | tf_op jit(solution)/shard_map/ppermute | solution.py:198
  80.1 50.6 %collective-permute-start.5 = (bf16[8,2,96,128]{3,2,1,0:T(8,128)(2,1)}, bf16[8,2,96,128]{3,2,1,0:T(8,128)(2,1)S(1)}, u32[]{:S(2)}, u32[]{:S(2)}) collective-permute-start(bf16[8,2,96,128]{3,2,1,0:T(8,128)(2,1)} %get-tuple-element.63), channel_id=1, source_target_pairs={{24,0},{32,8},{40,16},{48,24},{56,32},{64,40},{72,48},{80,56},{88,... | collective-permute-start | bytes 1179656 | tf_op jit(solution)/shard_map/ppermute | solution.py:198
  82.0 48.7 %collective-permute-start.6 = (bf16[8,2,96,128]{3,2,1,0:T(8,128)(2,1)}, bf16[8,2,96,128]{3,2,1,0:T(8,128)(2,1)S(1)}, u32[]{:S(2)}, u32[]{:S(2)}) collective-permute-start(bf16[8,2,96,128]{3,2,1,0:T(8,128)(2,1)} %get-tuple-element.64), channel_id=1, source_target_pairs={{16,0},{24,8},{32,16},{40,24},{48,32},{56,40},{64,48},{72,56},{80,... | collective-permute-start | bytes 1179656 | tf_op jit(solution)/shard_map/ppermute | solution.py:198
  84.2 46.5 %collective-permute-start.7 = (bf16[8,2,96,128]{3,2,1,0:T(8,128)(2,1)}, bf16[8,2,96,128]{3,2,1,0:T(8,128)(2,1)S(1)}, u32[]{:S(2)}, u32[]{:S(2)}) collective-permute-start(bf16[8,2,96,128]{3,2,1,0:T(8,128)(2,1)} %get-tuple-element.65), channel_id=1, source_target_pairs={{8,0},{16,8},{24,16},{32,24},{40,32},{48,40},{56,48},{64,56},{72,6... | collective-permute-start | bytes 1179656 | tf_op jit(solution)/shard_map/ppermute | solution.py:198
  88.2 42.5 %copy-start = (f32[8,2,96,128]{3,2,1,0:T(8,128)S(1)}, f32[8,2,96,128]{3,2,1,0:T(8,128)}, u32[]{:S(2)}) copy-start(f32[8,2,96,128]{3,2,1,0:T(8,128)} %get-tuple-element.68.mine_ref) | copy-start | bytes 2359300
  88.2 42.5 %copy-start.1 = (bf16[8,2,96,128]{3,2,1,0:T(8,128)(2,1)S(1)}, bf16[8,2,96,128]{3,2,1,0:T(8,128)(2,1)}, u32[]{:S(2)}) copy-start(bf16[8,2,96,128]{3,2,1,0:T(8,128)(2,1)} %get-tuple-element.67.od_ref) | copy-start | bytes 1179652
  131.9 6.1 %copy-start.7 = (bf16[32,96,128]{2,1,0:T(8,128)(2,1)S(1)}, bf16[32,96,128]{2,1,0:T(8,128)(2,1)}, u32[]{:S(2)}) copy-start(bf16[32,96,128]{2,1,0:T(8,128)(2,1)} %get-tuple-element.74) | copy-start | bytes 2359300
  131.9 29.0 %all-to-all-start.3 = ((bf16[32,2,96,128]{3,2,1,0:T(8,128)(2,1)}), bf16[32,2,96,128]{3,2,1,0:T(8,128)(2,1)S(1)}, u32[]{:S(2)}, u32[]{:S(2)}) async-start(bf16[32,2,96,128]{3,2,1,0:T(8,128)(2,1)} %get-tuple-element.73), calls=%async_computation.3 | async-start | bytes 3145728 | tf_op jit(solution)/shard_map/all_to_all | solution.py:194
  138.0 22.9 %collective-permute-start.8 = (bf16[32,96,128]{2,1,0:T(8,128)(2,1)S(1)}, bf16[32,96,128]{2,1,0:T(8,128)(2,1)S(1)}, u32[]{:S(2)}, u32[]{:S(2)}) collective-permute-start(bf16[32,96,128]{2,1,0:T(8,128)(2,1)S(1)} %copy-done.7), channel_id=1, source_target_pairs={{32,0},{64,32},{96,64},{33,1},{65,33},{97,65},{34,2},{66,34},{98,6... | collective-permute-start | bytes 2359304 | tf_op jit(solution)/shard_map/ppermute | solution.py:198
  139.9 37.5 %collective-permute-start.9 = (bf16[32,96,128]{2,1,0:T(8,128)(2,1)}, bf16[32,96,128]{2,1,0:T(8,128)(2,1)}, u32[]{:S(2)}, u32[]{:S(2)}) collective-permute-start(bf16[32,96,128]{2,1,0:T(8,128)(2,1)} %get-tuple-element.81), channel_id=1, source_target_pairs={{32,0},{64,32},{96,64},{33,1},{65,33},{97,65},{34,2},{66,34},{98,6... | collective-permute-start | bytes 2359304 | tf_op jit(solution)/shard_map/ppermute | solution.py:198
  160.9 16.5 %copy-start.4 = (bf16[32,96,128]{2,1,0:T(8,128)(2,1)}, bf16[32,96,128]{2,1,0:T(8,128)(2,1)S(1)}, u32[]{:S(2)}) copy-start(bf16[32,96,128]{2,1,0:T(8,128)(2,1)S(1)} %collective-permute-done.8.k_ref) | copy-start | bytes 2359300
  160.9 19.9 %all-to-all-start.4 = ((bf16[8,4,96,128]{3,2,1,0:T(8,128)(2,1)}), bf16[8,4,96,128]{3,2,1,0:T(8,128)(2,1)S(1)}, u32[]{:S(2)}, u32[]{:S(2)}) async-start(bf16[8,4,96,128]{3,2,1,0:T(8,128)(2,1)} %finish.1), calls=%async_computation.4 | async-start | bytes 1572864 | tf_op jit(solution)/shard_map/all_to_all | solution.py:194
  180.8 28.1 %all-to-all-start.5 = ((bf16[32,2,96,128]{3,2,1,0:T(8,128)(2,1)}), bf16[32,2,96,128]{3,2,1,0:T(8,128)(2,1)}, u32[]{:S(2)}, u32[]{:S(2)}) async-start(bf16[32,2,96,128]{3,2,1,0:T(8,128)(2,1)} %combine.1), calls=%async_computation.5 | async-start | bytes 3145728 | tf_op jit(solution)/shard_map/all_to_all | solution.py:194
  (1 other events, 0.9 us)
where the time goes:
time: 216 us; the launch traced here: 212 us
  waiting for transfers between devices  77.5 us (36%)
  Pallas kernels  70.9 us (33%)
  starting transfers between devices  60.3 us (28%)
    pallas_call x1, Pallas kernels, main_heads(): pl.pallas_call(main_kernel, out_shape=(bf(n, 2), bf(n), bf(n), bf(n, 2)),...  42.4 us
    ppermute x8, waiting for transfers between devices, shifted(): lax.ppermute(x, axes, [(i - distance, i) for i in range(size) if 0 <= i -...  40.6 us
    all_to_all x6, starting transfers between devices, exchange(): return lax.all_to_all(x, axes, 0, 0, tiled=True)  38.4 us
    all_to_all x6, waiting for transfers between devices, exchange(): return lax.all_to_all(x, axes, 0, 0, tiled=True)  35.4 us
    ppermute x8, starting transfers between devices, shifted(): lax.ppermute(x, axes, [(i - distance, i) for i in range(size) if 0 <= i -...  21.2 us
    pallas_call x5, Pallas kernels, moved(): pl.pallas_call(kernel, out_shape=tuple(out_shape), in_specs=[VMEM] * len(...  13.6 us
    pallas_call x1, Pallas kernels, fifth_head(): pl.pallas_call(fifth_kernel, out_shape=(bf(ULY, 2), jax.ShapeDtypeStruct(...  12.5 us
  transfers between devices with their start and end apart: 16, of which 8 were waited for; matrix products, arithmetic and copies ran while one was open for 1% of the time, Pallas kernels for 30%

commit v1 on v0

--- a/solution.py
+++ b/solution.py
@@ -30,15 +30,19 @@
     return lax.dot_general(a, b, (((ca,), (cb,)), ((), ())), preferred_element_type=F32)
 
 
-def attend(allowed, gi, q, g, od_ref, k_s, v_s, kt_s, vt_s, dk_s, dv_s, s_s, p_s):
+def attend(allowed, gi, q, g, od_ref, k_s, v_s, kt_s, vt_s, dk_s, dv_s, s_s, p_s, d_s):
     top = jnp.full((8, GROUP), -jnp.inf, F32)
+    tops = [top[:, :GROUP // 3]] * 3
     for c in range(WINDOW):
-        s = dot(k_s[gi + c], q, 1, 1)
-        s_s[c] = s
-        best = jnp.max(s.reshape(GROUP // 8, 8, GROUP), axis=0)
-        if c < WINDOW - 1:
-            best = jnp.where(allowed(c), best, -jnp.inf)
-        top = jnp.maximum(top, best)
+        for i in range(3):
+            part = slice(i * GROUP // 3, (i + 1) * GROUP // 3)
+            s = dot(k_s[gi + c], q[part], 1, 1)
+            s_s[c, :, part] = s
+            best = jnp.max(s.reshape(GROUP // 8, 8, GROUP // 3), axis=0)
+            if c < WINDOW - 1:
+                best = jnp.where(allowed(c), best, -jnp.inf)
+            tops[i] = jnp.maximum(tops[i], best)
+    top = jnp.concatenate(tops, axis=1)
     top = jnp.max(top, axis=0, keepdims=True)
     for c in range(WINDOW):
         base = top if c == WINDOW - 1 else jnp.where(allowed(c), top, 1e30)
@@ -55,15 +59,15 @@
     dp = dot(v_s[gi], g_tb)
     for c in range(WINDOW):
         pb = p_s[c]
-        ds = (pb.astype(F32) * (dp - row_dot)).astype(BF)
+        d_s[c] = (pb.astype(F32) * (dp - row_dot)).astype(BF)
         if c < WINDOW - 1:
             dp = dot(v_s[gi + c + 1], g_tb)
             dv_s[gi + c] += dot(pb, g_b)
-            dk_s[gi + c] += dot(ds, q)
+            dk_s[gi + c] += dot(d_s[c], q)
         else:
             dv_s[gi + c] = dot(pb, g_b)
-            dk_s[gi + c] = dot(ds, q)
-        dq_t = dq_t + dot(kt_s[gi + c], ds)
+            dk_s[gi + c] = dot(d_s[c], q)
+    dq_t = dot(jnp.concatenate([kt_s[gi + c] for c in range(WINDOW)], axis=1), d_s[...].reshape(WINDOW * GROUP, GROUP))
     od_ref[:, 1] = blocks((dq_t * FACTOR).T.astype(BF))
 
 
@@ -85,7 +89,7 @@
 
 
 def main_kernel(pos_ref, qg_ref, prev_ref, own_ref, od_ref, back_k_ref, back_v_ref, mine_ref,
-                k_s, v_s, kt_s, vt_s, dk_s, dv_s, s_s, p_s):
+                k_s, v_s, kt_s, vt_s, dk_s, dv_s, s_s, p_s, d_s):
     gi = pl.program_id(0)
     z = pos_ref[0]
 
@@ -99,7 +103,7 @@
         dv_s[:QUAD] = jnp.zeros((QUAD, GROUP, HEAD_DIM), F32)
 
     attend(lambda c: (z > 0) | (gi + c >= QUAD), gi, flat(qg_ref[:, 0]), flat(qg_ref[:, 1]), od_ref,
-           k_s, v_s, kt_s, vt_s, dk_s, dv_s, s_s, p_s)
+           k_s, v_s, kt_s, vt_s, dk_s, dv_s, s_s, p_s, d_s)
     back_k_ref[...] = blocks((dk_s[gi] * FACTOR).astype(BF))
     back_v_ref[...] = blocks(dv_s[gi].astype(BF))
 
@@ -112,13 +116,13 @@
 
 
 def fifth_kernel(flag_ref, all_ref, prev_ref, side_ref, core_ref, od_ref, mine_ref, b4_ref, b3_ref, b2_ref, b1_ref,
-                 k_s, v_s, kt_s, vt_s, dk_s, dv_s, s_s, p_s):
+                 k_s, v_s, kt_s, vt_s, dk_s, dv_s, s_s, p_s, d_s):
     for c, ref in enumerate((prev_ref, side_ref, core_ref.at[0], core_ref.at[1], all_ref.at[:, 2:4])):
         load_chunk(ref, c, k_s, v_s, kt_s, vt_s)
     dk_s[:QUAD] = jnp.zeros((QUAD, GROUP, HEAD_DIM), F32)
     dv_s[:QUAD] = jnp.zeros((QUAD, GROUP, HEAD_DIM), F32)
     attend(lambda c: flag_ref[c] > 0, 0, flat(all_ref[:, 0]), flat(all_ref[:, 1]), od_ref,
-           k_s, v_s, kt_s, vt_s, dk_s, dv_s, s_s, p_s)
+           k_s, v_s, kt_s, vt_s, dk_s, dv_s, s_s, p_s, d_s)
     mine_ref[:, 0] = blocks(dk_s[WINDOW - 1] * FACTOR)
     mine_ref[:, 1] = blocks(dv_s[WINDOW - 1])
     far = jnp.where(flag_ref[4] == 0, 2, 3)
@@ -136,6 +140,7 @@
         pltpu.VMEM((chunks, GROUP, HEAD_DIM), F32),
         pltpu.VMEM((chunks, GROUP, HEAD_DIM), F32),
         pltpu.VMEM((WINDOW, GROUP, GROUP), F32),
+        pltpu.VMEM((WINDOW, GROUP, GROUP), BF),
         pltpu.VMEM((WINDOW, GROUP, GROUP), BF),
     ]
 

time: 216 us -> 215 us (level)
  no operation moved by 1% of the time
where the time goes in v1:
time: 215 us; the launch traced here: 212 us
  waiting for transfers between devices  77.8 us (36%)
  Pallas kernels  70.5 us (33%)
  starting transfers between devices  59.9 us (28%)
    pallas_call x1, Pallas kernels, main_heads(): pl.pallas_call(main_kernel, out_shape=(bf(n, 2), bf(n), bf(n), bf(n, 2)),...  42.4 us
    ppermute x8, waiting for transfers between devices, shifted(): lax.ppermute(x, axes, [(i - distance, i) for i in range(size) if 0 <= i -...  40.9 us
    all_to_all x6, starting transfers between devices, exchange(): return lax.all_to_all(x, axes, 0, 0, tiled=True)  38.1 us
    all_to_all x6, waiting for transfers between devices, exchange(): return lax.all_to_all(x, axes, 0, 0, tiled=True)  35.4 us
    ppermute x8, starting transfers between devices, shifted(): lax.ppermute(x, axes, [(i - distance, i) for i in range(size) if 0 <= i -...  21.2 us
    pallas_call x5, Pallas kernels, moved(): pl.pallas_call(kernel, out_shape=tuple(out_shape), in_specs=[VMEM] * len(...  13.6 us
    pallas_call x1, Pallas kernels, fifth_head(): pl.pallas_call(fifth_kernel, out_shape=(bf(ULY, 2), jax.ShapeDtypeStruct(...  12.2 us
  transfers between devices with their start and end apart: 16, of which 8 were waited for; matrix products, arithmetic and copies ran while one was open for 1% of the time, Pallas kernels for 30%

profile of v1, /device:TPU:34, one launch (start us, length us, event | category | flops | bytes accessed | tf_op | source)
XLA Modules:
  0.0 211.6 jit_solution(3523144438669249947)
XLA Ops:
  0.6 2.3 %pack_fifth.1 = bf16[8,4,96,128]{3,2,1,0:T(8,128)(2,1)} custom-call(bf16[96,5120]{1,0:T(8,128)(2,1)} %q_ref.3, bf16[96,5120]{1,0:T(8,128)(2,1)} %g_ref.3, bf16[96,5120]{1,0:T(8,128)(2,1)} %k_ref.3, bf16[96,5120]{1,0:T(8,128)(2,1)} %v_ref.3), custom_call_target="tpu_custom_call" | custom-call | bytes 2097152 | tf_op jit(solution)/shard_map/pack_fifth/pallas_call | solution.py:266
  2.9 6.0 %all-to-all-start = ((bf16[8,4,96,128]{3,2,1,0:T(8,128)(2,1)}), bf16[8,4,96,128]{3,2,1,0:T(8,128)(2,1)S(1)}, u32[]{:S(2)}, u32[]{:S(2)}) async-start(bf16[8,4,96,128]{3,2,1,0:T(8,128)(2,1)} %pack_fifth.1), calls=%async_computation | async-start | bytes 1572864 | tf_op jit(solution)/shard_map/all_to_all | solution.py:199
  9.0 4.3 %pack.1 = (bf16[32,2,96,128]{3,2,1,0:T(8,128)(2,1)}, bf16[32,2,96,128]{3,2,1,0:T(8,128)(2,1)}) custom-call(bf16[96,5120]{1,0:T(8,128)(2,1)} %q_ref.3, bf16[96,5120]{1,0:T(8,128)(2,1)} %g_ref.3, bf16[96,5120]{1,0:T(8,128)(2,1)} %k_ref.3, bf16[96,5120]{1,0:T(8,128)(2,1)} %v_ref.3), custom_call_target="tpu_custom_call" | custom-call | bytes 4194304 | tf_op jit(solution)/shard_map/pack/pallas_call | solution.py:249
  13.2 10.1 %all-to-all-done.all_ref = bf16[8,4,96,128]{3,2,1,0:T(8,128)(2,1)S(1)} async-done(((bf16[8,4,96,128]{3,2,1,0:T(8,128)(2,1)}), bf16[8,4,96,128]{3,2,1,0:T(8,128)(2,1)S(1)}, u32[]{:S(2)}, u32[]{:S(2)}) %all-to-all-start) | async-done | bytes 786464 | tf_op jit(solution)/shard_map/all_to_all | solution.py:199
  23.4 5.2 %all-to-all-start.1 = ((bf16[32,2,96,128]{3,2,1,0:T(8,128)(2,1)}), bf16[32,2,96,128]{3,2,1,0:T(8,128)(2,1)S(1)}, u32[]{:S(2)}, u32[]{:S(2)}) async-start(bf16[32,2,96,128]{3,2,1,0:T(8,128)(2,1)} %get-tuple-element.47), calls=%async_computation.1 | async-start | bytes 3145728 | tf_op jit(solution)/shard_map/all_to_all | solution.py:199
  28.6 3.8 %collective-permute-start.1 = (bf16[8,2,96,128]{3,2,1,0:T(8,128)(2,1)S(1)}, bf16[8,2,96,128]{3,2,1,0:T(8,128)(2,1)S(1)}, u32[]{:S(2)}, u32[]{:S(2)}) collective-permute-start(bf16[8,2,96,128]{3,2,1,0:T(8,128)(2,1)S(1)} %slice.3), channel_id=1, source_target_pairs={{0,32},{32,64},{64,96},{1,33},{33,65},{65,97},{2,34},{34,66},{66,9... | collective-permute-start | bytes 1179656 | tf_op jit(solution)/shard_map/ppermute | solution.py:203
  32.4 9.2 %collective-permute-done.1.prev_ref = bf16[8,2,96,128]{3,2,1,0:T(8,128)(2,1)S(1)} collective-permute-done((bf16[8,2,96,128]{3,2,1,0:T(8,128)(2,1)S(1)}, bf16[8,2,96,128]{3,2,1,0:T(8,128)(2,1)S(1)}, u32[]{:S(2)}, u32[]{:S(2)}) %collective-permute-start.1) | collective-permute-done | bytes 393248 | tf_op jit(solution)/shard_map/ppermute | solution.py:203
  42.8 6.3 %all-to-all-done.1.own_ref = bf16[32,2,96,128]{3,2,1,0:T(8,128)(2,1)S(1)} async-done(((bf16[32,2,96,128]{3,2,1,0:T(8,128)(2,1)}), bf16[32,2,96,128]{3,2,1,0:T(8,128)(2,1)S(1)}, u32[]{:S(2)}, u32[]{:S(2)}) %all-to-all-start.1) | async-done | bytes 1572896 | tf_op jit(solution)/shard_map/all_to_all | solution.py:199
  49.1 3.8 %collective-permute-start = (bf16[32,2,96,128]{3,2,1,0:T(8,128)(2,1)S(1)}, bf16[32,2,96,128]{3,2,1,0:T(8,128)(2,1)}, u32[]{:S(2)}, u32[]{:S(2)}) collective-permute-start(bf16[32,2,96,128]{3,2,1,0:T(8,128)(2,1)S(1)} %all-to-all-done.1.own_ref), channel_id=1, source_target_pairs={{0,32},{32,64},{64,96},{1,33},{33,65},{65,97},{2,34},{34,66},{66,9... | collective-permute-start | bytes 4718600 | tf_op jit(solution)/shard_map/ppermute | solution.py:203
  52.9 7.9 %all-to-all-start.2 = ((bf16[32,2,96,128]{3,2,1,0:T(8,128)(2,1)}), bf16[32,2,96,128]{3,2,1,0:T(8,128)(2,1)}, u32[]{:S(2)}, u32[]{:S(2)}) async-start(bf16[32,2,96,128]{3,2,1,0:T(8,128)(2,1)} %get-tuple-element.49), calls=%async_computation.2 | async-start | bytes 3145728 | tf_op jit(solution)/shard_map/all_to_all | solution.py:199
  64.4 12.2 %fifth_head.1 = (bf16[8,2,96,128]{3,2,1,0:T(8,128)(2,1)}, f32[8,2,96,128]{3,2,1,0:T(8,128)}, bf16[8,2,96,128]{3,2,1,0:T(8,128)(2,1)}, bf16[8,2,96,128]{3,2,1,0:T...) custom-call(s32[5]{0:T(128)} %stack.29.flag_ref, bf16[8,4,96,128]{3,2,1,0:T(8,128)(2,1)} %copy-done.2, ...), custom_call_target="tpu_custom_call" | custom-call | flops 4529848320 | bytes 5000000 | tf_op jit(solution)/shard_map/fifth_head/pallas_call | solution.py:186
  76.6 3.1 %collective-permute-start.4 = (bf16[8,2,96,128]{3,2,1,0:T(8,128)(2,1)}, bf16[8,2,96,128]{3,2,1,0:T(8,128)(2,1)S(1)}, u32[]{:S(2)}, u32[]{:S(2)}) collective-permute-start(bf16[8,2,96,128]{3,2,1,0:T(8,128)(2,1)} %get-tuple-element.62), channel_id=1, source_target_pairs={{32,0},{40,8},{48,16},{56,24},{64,32},{72,40},{80,48},{88,56},{96,... | collective-permute-start | bytes 1179656 | tf_op jit(solution)/shard_map/ppermute | solution.py:203
  81.7 2.2 %collective-permute-start.6 = (bf16[8,2,96,128]{3,2,1,0:T(8,128)(2,1)}, bf16[8,2,96,128]{3,2,1,0:T(8,128)(2,1)S(1)}, u32[]{:S(2)}, u32[]{:S(2)}) collective-permute-start(bf16[8,2,96,128]{3,2,1,0:T(8,128)(2,1)} %get-tuple-element.64), channel_id=1, source_target_pairs={{16,0},{24,8},{32,16},{40,24},{48,32},{56,40},{64,48},{72,56},{80,... | collective-permute-start | bytes 1179656 | tf_op jit(solution)/shard_map/ppermute | solution.py:203
  83.9 2.4 %collective-permute-start.7 = (bf16[8,2,96,128]{3,2,1,0:T(8,128)(2,1)}, bf16[8,2,96,128]{3,2,1,0:T(8,128)(2,1)S(1)}, u32[]{:S(2)}, u32[]{:S(2)}) collective-permute-start(bf16[8,2,96,128]{3,2,1,0:T(8,128)(2,1)} %get-tuple-element.65), channel_id=1, source_target_pairs={{8,0},{16,8},{24,16},{32,24},{40,32},{48,40},{56,48},{64,56},{72,6... | collective-permute-start | bytes 1179656 | tf_op jit(solution)/shard_map/ppermute | solution.py:203
  86.3 1.9 collective-permute-done.prev_ref
  88.2 42.4 %main_heads.1 = (bf16[32,2,96,128]{3,2,1,0:T(8,128)(2,1)}, bf16[32,96,128]{2,1,0:T(8,128)(2,1)}, bf16[32,96,128]{2,1,0:T(8,128)(2,1)}, bf16[32,2,96,128]{3,2,1,0:T(8,128)(2,1)}) custom-call(s32[1]{0:T(128)} %bitcast.pos_ref, bf16[32,2,96,128]{3,2,1,0:T(8,128)(2,1)} %all-to-all-done.2.qg_ref, bf16[32,2,96,128]{3,2,1,0:T(8,128)(2,1)} %collective-permute-done.prev_ref, ...), custom_call_target="tpu_custom_call" | custom-call | flops 18119393280 | bytes 20000000 | tf_op jit(solution)/shard_map/main_heads/pallas_call | solution.py:172
  131.8 5.8 %all-to-all-start.3 = ((bf16[32,2,96,128]{3,2,1,0:T(8,128)(2,1)}), bf16[32,2,96,128]{3,2,1,0:T(8,128)(2,1)S(1)}, u32[]{:S(2)}, u32[]{:S(2)}) async-start(bf16[32,2,96,128]{3,2,1,0:T(8,128)(2,1)} %get-tuple-element.73), calls=%async_computation.3 | async-start | bytes 3145728 | tf_op jit(solution)/shard_map/all_to_all | solution.py:199
  141.5 19.0 %collective-permute-done.8.k_ref = bf16[32,96,128]{2,1,0:T(8,128)(2,1)S(1)} collective-permute-done((bf16[32,96,128]{2,1,0:T(8,128)(2,1)S(1)}, bf16[32,96,128]{2,1,0:T(8,128)(2,1)S(1)}, u32[]{:S(2)}, u32[]{:S(2)}) %collective-permute-start.8) | collective-permute-done | bytes 786464 | tf_op jit(solution)/shard_map/ppermute | solution.py:203
  160.5 5.8 %all-to-all-start.4 = ((bf16[8,4,96,128]{3,2,1,0:T(8,128)(2,1)}), bf16[8,4,96,128]{3,2,1,0:T(8,128)(2,1)S(1)}, u32[]{:S(2)}, u32[]{:S(2)}) async-start(bf16[8,4,96,128]{3,2,1,0:T(8,128)(2,1)} %finish.1), calls=%async_computation.4 | async-start | bytes 1572864 | tf_op jit(solution)/shard_map/all_to_all | solution.py:199
  166.2 10.7 %collective-permute-done.9.v_ref = bf16[32,96,128]{2,1,0:T(8,128)(2,1)} collective-permute-done((bf16[32,96,128]{2,1,0:T(8,128)(2,1)}, bf16[32,96,128]{2,1,0:T(8,128)(2,1)}, u32[]{:S(2)}, u32[]{:S(2)}) %collective-permute-start.9) | collective-permute-done | bytes 786464 | tf_op jit(solution)/shard_map/ppermute | solution.py:203
  177.0 3.4 %combine.1 = bf16[32,2,96,128]{3,2,1,0:T(8,128)(2,1)} custom-call(bf16[32,2,96,128]{3,2,1,0:T(8,128)(2,1)} %get-tuple-element.79.mine_ref, bf16[32,96,128]{2,1,0:T(8,128)(2,1)} %copy-done.4, bf16[32,96,128]{2,1,0:T(8,128)(2,1)} %collective-permute-done.9.v_ref), custom_call_target="tpu_custom_call" | custom-call | bytes 4194304 | tf_op jit(solution)/shard_map/combine/pallas_call | solution.py:249
  180.4 7.4 %all-to-all-start.5 = ((bf16[32,2,96,128]{3,2,1,0:T(8,128)(2,1)}), bf16[32,2,96,128]{3,2,1,0:T(8,128)(2,1)}, u32[]{:S(2)}, u32[]{:S(2)}) async-start(bf16[32,2,96,128]{3,2,1,0:T(8,128)(2,1)} %combine.1), calls=%async_computation.5 | async-start | bytes 3145728 | tf_op jit(solution)/shard_map/all_to_all | solution.py:199
  189.5 19.0 %all-to-all-done.5.main_ref = bf16[32,2,96,128]{3,2,1,0:T(8,128)(2,1)} async-done(((bf16[32,2,96,128]{3,2,1,0:T(8,128)(2,1)}), bf16[32,2,96,128]{3,2,1,0:T(8,128)(2,1)}, u32[]{:S(2)}, u32[]{:S(2)}) %all-to-all-start.5) | async-done | bytes 1572896 | tf_op jit(solution)/shard_map/all_to_all | solution.py:199
  208.5 3.1 %unpack.3 = (bf16[96,5120]{1,0:T(8,128)(2,1)}, bf16[96,5120]{1,0:T(8,128)(2,1)}) custom-call(bf16[32,2,96,128]{3,2,1,0:T(8,128)(2,1)} %all-to-all-done.5.main_ref, bf16[8,4,96,128]{3,2,1,0:T(8,128)(2,1)S(1)} %all-to-all-done.4.fifth_ref), custom_call_target="tpu_custom_call" | custom-call | bytes 4194304 | tf_op jit(solution)/shard_map/unpack/pallas_call | solution.py:249
  (38 shorter events, 13.4 us)
Async XLA Ops:
  2.9 20.4 %all-to-all-start = ((bf16[8,4,96,128]{3,2,1,0:T(8,128)(2,1)}), bf16[8,4,96,128]{3,2,1,0:T(8,128)(2,1)S(1)}, u32[]{:S(2)}, u32[]{:S(2)}) async-start(bf16[8,4,96,128]{3,2,1,0:T(8,128)(2,1)} %pack_fifth.1), calls=%async_computation | async-start | bytes 1572864 | tf_op jit(solution)/shard_map/all_to_all | solution.py:199
  23.4 18.3 %copy-start.2 = (bf16[8,4,96,128]{3,2,1,0:T(8,128)(2,1)}, bf16[8,4,96,128]{3,2,1,0:T(8,128)(2,1)S(1)}, u32[]{:S(2)}) copy-start(bf16[8,4,96,128]{3,2,1,0:T(8,128)(2,1)S(1)} %all-to-all-done.all_ref) | copy-start | bytes 2359300
  23.4 25.8 %all-to-all-start.1 = ((bf16[32,2,96,128]{3,2,1,0:T(8,128)(2,1)}), bf16[32,2,96,128]{3,2,1,0:T(8,128)(2,1)S(1)}, u32[]{:S(2)}, u32[]{:S(2)}) async-start(bf16[32,2,96,128]{3,2,1,0:T(8,128)(2,1)} %get-tuple-element.47), calls=%async_computation.1 | async-start | bytes 3145728 | tf_op jit(solution)/shard_map/all_to_all | solution.py:199
  28.6 13.1 %collective-permute-start.1 = (bf16[8,2,96,128]{3,2,1,0:T(8,128)(2,1)S(1)}, bf16[8,2,96,128]{3,2,1,0:T(8,128)(2,1)S(1)}, u32[]{:S(2)}, u32[]{:S(2)}) collective-permute-start(bf16[8,2,96,128]{3,2,1,0:T(8,128)(2,1)S(1)} %slice.3), channel_id=1, source_target_pairs={{0,32},{32,64},{64,96},{1,33},{33,65},{65,97},{2,34},{34,66},{66,9... | collective-permute-start | bytes 1179656 | tf_op jit(solution)/shard_map/ppermute | solution.py:203
  41.6 11.3 %copy-start.5 = (bf16[8,2,96,128]{3,2,1,0:T(8,128)(2,1)}, bf16[8,2,96,128]{3,2,1,0:T(8,128)(2,1)S(1)}, u32[]{:S(2)}) copy-start(bf16[8,2,96,128]{3,2,1,0:T(8,128)(2,1)S(1)} %collective-permute-done.1.prev_ref) | copy-start | bytes 1179652
  42.5 18.3 %collective-permute-start.2 = (bf16[8,2,96,128]{3,2,1,0:T(8,128)(2,1)}, bf16[8,2,96,128]{3,2,1,0:T(8,128)(2,1)S(1)}, u32[]{:S(2)}, u32[]{:S(2)}) collective-permute-start(bf16[8,2,96,128]{3,2,1,0:T(8,128)(2,1)} %get-tuple-element.89), channel_id=1, source_target_pairs={{0,16},{16,0},{1,17},{17,1},{2,18},{18,2},{3,19},{19,3},{4,20},{20... | collective-permute-start | bytes 1179656 | tf_op jit(solution)/shard_map/ppermute | solution.py:288
  49.1 3.8 %copy-start.3 = (bf16[32,2,96,128]{3,2,1,0:T(8,128)(2,1)}, bf16[32,2,96,128]{3,2,1,0:T(8,128)(2,1)S(1)}, u32[]{:S(2)}) copy-start(bf16[32,2,96,128]{3,2,1,0:T(8,128)(2,1)S(1)} %all-to-all-done.1.own_ref) | copy-start | bytes 4718596
  49.1 39.1 %collective-permute-start = (bf16[32,2,96,128]{3,2,1,0:T(8,128)(2,1)S(1)}, bf16[32,2,96,128]{3,2,1,0:T(8,128)(2,1)}, u32[]{:S(2)}, u32[]{:S(2)}) collective-permute-start(bf16[32,2,96,128]{3,2,1,0:T(8,128)(2,1)S(1)} %all-to-all-done.1.own_ref), channel_id=1, source_target_pairs={{0,32},{32,64},{64,96},{1,33},{33,65},{65,97},{2,34},{34,66},{66,9... | collective-permute-start | bytes 4718600 | tf_op jit(solution)/shard_map/ppermute | solution.py:203
  52.9 33.3 %all-to-all-start.2 = ((bf16[32,2,96,128]{3,2,1,0:T(8,128)(2,1)}), bf16[32,2,96,128]{3,2,1,0:T(8,128)(2,1)}, u32[]{:S(2)}, u32[]{:S(2)}) async-start(bf16[32,2,96,128]{3,2,1,0:T(8,128)(2,1)} %get-tuple-element.49), calls=%async_computation.2 | async-start | bytes 3145728 | tf_op jit(solution)/shard_map/all_to_all | solution.py:199
  60.9 2.6 %copy-start.6 = (bf16[8,2,96,128]{3,2,1,0:T(8,128)(2,1)}, bf16[8,2,96,128]{3,2,1,0:T(8,128)(2,1)S(1)}, u32[]{:S(2)}) copy-start(bf16[8,2,96,128]{3,2,1,0:T(8,128)(2,1)S(1)} %collective-permute-done.2.side_ref) | copy-start | bytes 1179652
  61.0 2.5 %collective-permute-start.3 = (bf16[2,8,2,96,128]{4,3,2,1,0:T(8,128)(2,1)S(1)}, bf16[2,8,2,96,128]{4,3,2,1,0:T(8,128)(2,1)S(1)}, u32[]{:S(2)}, u32[]{:S(2)}) collective-permute-start(bf16[2,8,2,96,128]{4,3,2,1,0:T(8,128)(2,1)S(1)} %pad_maximum_fusion), channel_id=1, source_target_pairs={{0,8},{8,0},{1,9},{9,1},{2,10},{10,2},{3,11},{11,3},{4,12},{12,4},... | collective-permute-start | bytes 2359304 | tf_op jit(solution)/shard_map/ppermute | solution.py:288
  76.6 54.0 %collective-permute-start.4 = (bf16[8,2,96,128]{3,2,1,0:T(8,128)(2,1)}, bf16[8,2,96,128]{3,2,1,0:T(8,128)(2,1)S(1)}, u32[]{:S(2)}, u32[]{:S(2)}) collective-permute-start(bf16[8,2,96,128]{3,2,1,0:T(8,128)(2,1)} %get-tuple-element.62), channel_id=1, source_target_pairs={{32,0},{40,8},{48,16},{56,24},{64,32},{72,40},{80,48},{88,56},{96,... | collective-permute-start | bytes 1179656 | tf_op jit(solution)/shard_map/ppermute | solution.py:203
  79.7 50.9 %collective-permute-start.5 = (bf16[8,2,96,128]{3,2,1,0:T(8,128)(2,1)}, bf16[8,2,96,128]{3,2,1,0:T(8,128)(2,1)S(1)}, u32[]{:S(2)}, u32[]{:S(2)}) collective-permute-start(bf16[8,2,96,128]{3,2,1,0:T(8,128)(2,1)} %get-tuple-element.63), channel_id=1, source_target_pairs={{24,0},{32,8},{40,16},{48,24},{56,32},{64,40},{72,48},{80,56},{88,... | collective-permute-start | bytes 1179656 | tf_op jit(solution)/shard_map/ppermute | solution.py:203
  81.7 49.0 %collective-permute-start.6 = (bf16[8,2,96,128]{3,2,1,0:T(8,128)(2,1)}, bf16[8,2,96,128]{3,2,1,0:T(8,128)(2,1)S(1)}, u32[]{:S(2)}, u32[]{:S(2)}) collective-permute-start(bf16[8,2,96,128]{3,2,1,0:T(8,128)(2,1)} %get-tuple-element.64), channel_id=1, source_target_pairs={{16,0},{24,8},{32,16},{40,24},{48,32},{56,40},{64,48},{72,56},{80,... | collective-permute-start | bytes 1179656 | tf_op jit(solution)/shard_map/ppermute | solution.py:203
  83.9 46.8 %collective-permute-start.7 = (bf16[8,2,96,128]{3,2,1,0:T(8,128)(2,1)}, bf16[8,2,96,128]{3,2,1,0:T(8,128)(2,1)S(1)}, u32[]{:S(2)}, u32[]{:S(2)}) collective-permute-start(bf16[8,2,96,128]{3,2,1,0:T(8,128)(2,1)} %get-tuple-element.65), channel_id=1, source_target_pairs={{8,0},{16,8},{24,16},{32,24},{40,32},{48,40},{56,48},{64,56},{72,6... | collective-permute-start | bytes 1179656 | tf_op jit(solution)/shard_map/ppermute | solution.py:203
  88.2 42.4 %copy-start = (f32[8,2,96,128]{3,2,1,0:T(8,128)S(1)}, f32[8,2,96,128]{3,2,1,0:T(8,128)}, u32[]{:S(2)}) copy-start(f32[8,2,96,128]{3,2,1,0:T(8,128)} %get-tuple-element.68.mine_ref) | copy-start | bytes 2359300
  88.2 42.4 %copy-start.1 = (bf16[8,2,96,128]{3,2,1,0:T(8,128)(2,1)S(1)}, bf16[8,2,96,128]{3,2,1,0:T(8,128)(2,1)}, u32[]{:S(2)}) copy-start(bf16[8,2,96,128]{3,2,1,0:T(8,128)(2,1)} %get-tuple-element.67.od_ref) | copy-start | bytes 1179652
  131.8 5.8 %copy-start.7 = (bf16[32,96,128]{2,1,0:T(8,128)(2,1)S(1)}, bf16[32,96,128]{2,1,0:T(8,128)(2,1)}, u32[]{:S(2)}) copy-start(bf16[32,96,128]{2,1,0:T(8,128)(2,1)} %get-tuple-element.74) | copy-start | bytes 2359300
  131.8 28.7 %all-to-all-start.3 = ((bf16[32,2,96,128]{3,2,1,0:T(8,128)(2,1)}), bf16[32,2,96,128]{3,2,1,0:T(8,128)(2,1)S(1)}, u32[]{:S(2)}, u32[]{:S(2)}) async-start(bf16[32,2,96,128]{3,2,1,0:T(8,128)(2,1)} %get-tuple-element.73), calls=%async_computation.3 | async-start | bytes 3145728 | tf_op jit(solution)/shard_map/all_to_all | solution.py:199
  137.6 22.9 %collective-permute-start.8 = (bf16[32,96,128]{2,1,0:T(8,128)(2,1)S(1)}, bf16[32,96,128]{2,1,0:T(8,128)(2,1)S(1)}, u32[]{:S(2)}, u32[]{:S(2)}) collective-permute-start(bf16[32,96,128]{2,1,0:T(8,128)(2,1)S(1)} %copy-done.7), channel_id=1, source_target_pairs={{32,0},{64,32},{96,64},{33,1},{65,33},{97,65},{34,2},{66,34},{98,6... | collective-permute-start | bytes 2359304 | tf_op jit(solution)/shard_map/ppermute | solution.py:203
  139.5 37.4 %collective-permute-start.9 = (bf16[32,96,128]{2,1,0:T(8,128)(2,1)}, bf16[32,96,128]{2,1,0:T(8,128)(2,1)}, u32[]{:S(2)}, u32[]{:S(2)}) collective-permute-start(bf16[32,96,128]{2,1,0:T(8,128)(2,1)} %get-tuple-element.81), channel_id=1, source_target_pairs={{32,0},{64,32},{96,64},{33,1},{65,33},{97,65},{34,2},{66,34},{98,6... | collective-permute-start | bytes 2359304 | tf_op jit(solution)/shard_map/ppermute | solution.py:203
  160.5 16.5 %copy-start.4 = (bf16[32,96,128]{2,1,0:T(8,128)(2,1)}, bf16[32,96,128]{2,1,0:T(8,128)(2,1)S(1)}, u32[]{:S(2)}) copy-start(bf16[32,96,128]{2,1,0:T(8,128)(2,1)S(1)} %collective-permute-done.8.k_ref) | copy-start | bytes 2359300
  160.5 19.9 %all-to-all-start.4 = ((bf16[8,4,96,128]{3,2,1,0:T(8,128)(2,1)}), bf16[8,4,96,128]{3,2,1,0:T(8,128)(2,1)S(1)}, u32[]{:S(2)}, u32[]{:S(2)}) async-start(bf16[8,4,96,128]{3,2,1,0:T(8,128)(2,1)} %finish.1), calls=%async_computation.4 | async-start | bytes 1572864 | tf_op jit(solution)/shard_map/all_to_all | solution.py:199
  180.4 28.1 %all-to-all-start.5 = ((bf16[32,2,96,128]{3,2,1,0:T(8,128)(2,1)}), bf16[32,2,96,128]{3,2,1,0:T(8,128)(2,1)}, u32[]{:S(2)}, u32[]{:S(2)}) async-start(bf16[32,2,96,128]{3,2,1,0:T(8,128)(2,1)} %combine.1), calls=%async_computation.5 | async-start | bytes 3145728 | tf_op jit(solution)/shard_map/all_to_all | solution.py:199
  (1 other events, 0.9 us)
